TPU v7x, 32 devices: a whole 2x2x4 slice. The times are simulated.
32 devices in a mesh: lat: 4 (over x, core), lon: 8 (over z, y).
Axes of the slice: x: 2, y: 2, z: 4, core: 2. Of those that a mesh axis runs over, the one named last changes fastest.
Arguments:
- cell_state: bfloat16 [4, 8, 512, 32, 64], P('lat', 'lon'), may hold values from -6 to 6
- remap_weight: bfloat16 [4, 8, 512, 64, 128], P('lat', 'lon'), may hold values from -0.75 to 0.75
- block_target: int32 [4, 8, 512], P('lat', 'lon'), may hold values from 0 to 255, as said below
- block_count: int32 [4, 8], P('lat', 'lon'), may hold values from 256 to 512, as said below
- border_state: bfloat16 [4, 8, 128, 32, 64], P('lat', 'lon'), may hold values from -6 to 6
- border_weight: bfloat16 [4, 8, 128, 64, 128], P('lat', 'lon'), may hold values from -0.75 to 0.75
- border_target: int32 [4, 8, 128], P('lat', 'lon'), may hold values from 0 to 63
- kernel_one: bfloat16 [7, 7, 32, 64], replicated, may hold values from -0.15625 to 0.15625
- bias_one: float32 [64], replicated, may hold values from -4 to 4
- gain_one: float32 [64], replicated, may hold values from 0.1 to 1.9
- kernel_two: bfloat16 [7, 7, 64, 128], replicated, may hold values from -0.109375 to 0.109375
- bias_two: float32 [128], replicated, may hold values from -4 to 4
- gain_two: float32 [128], replicated, may hold values from 0.1 to 1.9
Outputs:
- encoded: bfloat16 [256, 256, 128], P('lat', 'lon')
Inputs may be any that keep to these rules, and one draw needn't show every extreme that they name: `block_count`: slots below a device's count are live; the largest count is exactly 512 in every draw. `block_target`: on every device, slots 0 to 255 name each patch of the tile once, in an order drawn from the seed; later slots name patches at random.
All inputs are finite; a program needn't handle non-finite values.
Results may differ from a plain program's by a relative error of at most 0.0045.
Values may be sent and summed in bfloat16 or wider, within the bound.
A program may use at most 192 MiB of HBM per device.

v0:
```python
import functools

import jax
import jax.numpy as jnp
import numpy as np
from jax import lax
from jax.experimental import pallas as pl
from jax.experimental.pallas import tpu as pltpu
from jax.sharding import PartitionSpec as P

PH = 8
PW = 16
EDGE = 1
TH = 256
W = 128
PACK = 4
VMEM_LIMIT = 56 * 1024 * 1024
F32 = jnp.float32
BF16 = jnp.bfloat16


def params():
    return pltpu.CompilerParams(vmem_limit_bytes=VMEM_LIMIT)


def turn_states(s_ref, turned, distance):
    channels, _, block = s_ref.shape

    def body(i, _):
        for u in range(2):
            c = i * 2 + u
            v = s_ref[c]
            if block == distance * 2 and distance % 128 == 0:
                pair = jnp.concatenate([v[:, :distance], v[:, distance:]], axis=0)
            else:
                other = pltpu.roll(v.astype(F32), block - distance, 1).astype(BF16)
                pair = jnp.concatenate([v, other], axis=0)
            pair = pair.T.astype(F32)
            turned[pl.ds(c, pair.shape[0], stride=channels)] = pair
        return 0

    lax.fori_loop(0, channels // 2, body, 0)


def group_slots(g, distance):
    return (2 * g, 2 * g + distance, 2 * g + 1, 2 * g + 1 + distance)


def group_product(turned, w_ref, mask, g, channels, distance):
    start = pl.multiple_of(g * 2 * channels, 2 * channels)
    s = jnp.concatenate(
        [turned[pl.ds(start, channels)], turned[pl.ds(start + channels, channels)]], axis=1
    ).astype(BF16)
    lhs = jnp.concatenate([s] * PACK, axis=0) * mask
    rhs = jnp.concatenate([w_ref[slot] for slot in group_slots(g, distance)], axis=0)
    return jnp.dot(lhs, rhs, preferred_element_type=F32)


def slot_mask(channels, cells):
    row = lax.broadcasted_iota(jnp.int32, (PACK * channels, PACK * cells), 0) // channels
    col = lax.broadcasted_iota(jnp.int32, (PACK * channels, PACK * cells), 1) // cells
    return jnp.where(row == col, 1.0, 0.0).astype(BF16)


def add_groups(base, s_ref, w_ref, turned, store):
    channels, cells, block = s_ref.shape
    distance = block // 2
    turn_states(s_ref, turned, distance)
    mask = slot_mask(channels, cells)

    def body(i, _):
        for u in range(4):
            g = i * 4 + u
            prod = group_product(turned, w_ref, mask, g, channels, distance)
            for k, slot in enumerate(group_slots(g, distance)):
                store(base + slot, prod[k * channels : (k + 1) * channels])
        return 0

    lax.fori_loop(0, block // (4 * PACK), body, 0)


def border_kernel(target_ref, s_ref, w_ref, west_ref, east_ref, acc, turned):
    acc[...] = jnp.zeros_like(acc)

    def add(slot, value):
        acc[target_ref[slot]] += value

    add_groups(0, s_ref, w_ref, turned, add)
    half = west_ref.shape[0]
    west_ref[...] = acc[:half].astype(BF16)
    east_ref[...] = acc[half:].astype(BF16)


def border_sums(states, weights, targets, count):
    n, c, b = states.shape
    pixels = weights.shape[2]
    return pl.pallas_call(
        border_kernel,
        grid_spec=pltpu.PrefetchScalarGridSpec(
            num_scalar_prefetch=1,
            grid=(1,),
            in_specs=[
                pl.BlockSpec((c, b, n), lambda i, t: (0, 0, 0)),
                pl.BlockSpec((n, b, pixels), lambda i, t: (0, 0, 0)),
            ],
            out_specs=[pl.BlockSpec((count // 2, c, pixels), lambda i, t: (0, 0, 0))] * 2,
            scratch_shapes=[pltpu.VMEM((count, c, pixels), F32), pltpu.VMEM((n * c, 2 * b), F32)],
        ),
        out_shape=[jax.ShapeDtypeStruct((count // 2, c, pixels), BF16)] * 2,
        compiler_params=params(),
        name="border_sums",
    )(targets, states.transpose(1, 2, 0), weights)


def inner_kernel(first_steps, target_ref, live_ref, s_ref, w_ref, acc, turned):
    step = pl.program_id(0)
    base = step * s_ref.shape[2]

    @pl.when(step < first_steps)
    def _():
        def put(slot, value):
            acc[target_ref[slot]] = value

        add_groups(base, s_ref, w_ref, turned, put)

    @pl.when((step >= first_steps) & (base < live_ref[0]))
    def _():
        def add(slot, value):
            alive = jnp.where(slot < live_ref[0], 1.0, 0.0)
            acc[target_ref[slot]] += value * alive

        add_groups(base, s_ref, w_ref, turned, add)


def inner_sums(states, weights, targets, live, patches):
    n, c, b = states.shape
    pixels = weights.shape[2]
    block = patches
    return pl.pallas_call(
        functools.partial(inner_kernel, patches // block),
        grid_spec=pltpu.PrefetchScalarGridSpec(
            num_scalar_prefetch=2,
            grid=(n // block,),
            in_specs=[
                pl.BlockSpec((c, b, block), lambda i, t, l: (0, 0, i)),
                pl.BlockSpec((block, b, pixels), lambda i, t, l: (i, 0, 0)),
            ],
            out_specs=pl.BlockSpec((patches, c, pixels), lambda i, t, l: (0, 0, 0)),
            scratch_shapes=[pltpu.VMEM((block // 2 * c, 2 * b), F32)],
        ),
        out_shape=jax.ShapeDtypeStruct((patches, c, pixels), F32),
        compiler_params=params(),
        name="inner_sums",
    )(targets, live, states.transpose(1, 2, 0), weights)


def placement():
    j, ph, pw = np.meshgrid(np.arange(PACK), np.arange(PH), np.arange(PW), indexing="ij")
    f = (ph % 2) * 2 + pw % 2
    positions = PACK * PH * PW // 4
    rx2 = (pw // 2) % 2
    pos = ((rx2 * (PH // 2) + ph // 2) * PACK + j) * (PW // 4) + pw // 4
    table = np.zeros((PACK * PH * PW, 4 * positions), np.float32)
    table[np.arange(table.shape[0]), (f * positions + pos).ravel()] = 1.0
    return table


def field_kernel(cols, acc_ref, west_ref, east_ref, place_ref, out_ref):
    prows = out_ref.shape[0] // (PH // 4)
    channels = acc_ref.shape[1]
    wide = PACK * (PW // 4)
    rows = []
    for r in range(prows):
        for jg in range(cols // PACK):
            parts = []
            for j in range(PACK):
                col = jg * PACK + j
                v = acc_ref[r * cols + col]
                if col == 0:
                    v = v + west_ref[r].astype(F32)
                if col == cols - 1:
                    v = v + east_ref[r].astype(F32)
                parts.append(v.astype(BF16))
            rows.append(jnp.concatenate(parts, axis=1))
    moved = jnp.dot(jnp.concatenate(rows, axis=0), place_ref[...], preferred_element_type=F32)
    npos = moved.shape[1] // 4
    at = 0
    for r in range(prows):
        for jg in range(cols // PACK):
            part = moved[at : at + channels]
            at += channels
            stacked = jnp.concatenate([part[:, f * npos : (f + 1) * npos] for f in range(4)], axis=0)
            turned = stacked.astype(BF16).T
            for rx2 in range(2):
                for py in range(PH // 2):
                    start = (rx2 * (PH // 2) + py) * wide
                    lane = ((py % 2) * 2 + rx2) * 4 * channels
                    out_ref[
                        r * (PH // 4) + py // 2, jg * wide : (jg + 1) * wide, lane : lane + 4 * channels
                    ] = turned[start : start + wide]


def build_field(acc, west, east, patch_rows, patch_cols):
    _, c, pixels = acc.shape
    step = 4
    per = step * PH // 4
    place = jnp.asarray(placement(), BF16)
    return pl.pallas_call(
        functools.partial(field_kernel, patch_cols),
        grid=(patch_rows // step,),
        in_specs=[
            pl.BlockSpec((step * patch_cols, c, pixels), lambda i: (i, 0, 0)),
            pl.BlockSpec((step, c, pixels), lambda i: (i, 0, 0)),
            pl.BlockSpec((step, c, pixels), lambda i: (i, 0, 0)),
            pl.BlockSpec(place.shape, lambda i: (0, 0)),
        ],
        out_specs=pl.BlockSpec((per, patch_cols * PW // 4, 16 * c), lambda i: (i, 0, 0)),
        out_shape=jax.ShapeDtypeStruct((patch_rows * PH // 4, patch_cols * PW // 4, 16 * c), BF16),
        compiler_params=params(),
        name="field",
    )(acc, west, east, place)


def flip_lines(v, swap):
    pieces = [v[:, i : i + 128] for i in range(0, v.shape[1], 128)]
    half = len(pieces) // 2
    pieces = pieces[half:] + pieces[:half]
    if swap:
        pieces = [pltpu.roll(p, swap, 1) for p in pieces]
    return jnp.concatenate(pieces, axis=1)


def gelu(v):
    inner = np.float32(np.sqrt(2 / np.pi)) * (v + np.float32(0.044715) * (v * v * v))
    return 0.5 * v * (1.0 + jnp.tanh(inner))


def exchange_start(left, right, x_ref, col_e, col_w, send_e, send_w, recv_w, recv_e, lines, corner_w, corner_e, sems):
    nlat, nlon = lax.axis_size("lat"), lax.axis_size("lon")
    rows, cols, _ = x_ref.shape
    above = lines.shape[1]
    tile = corner_w.shape[2]
    send_sem, recv_sem = sems
    lat, lon = lax.axis_index("lat"), lax.axis_index("lon")
    is_top, is_bottom = (nlat - lat) // nlat, (lat + 1) // nlat
    west = (lat, (lon + nlon - 1) % nlon)
    east = (lat, (lon + 1) % nlon)

    def up(d):
        return (lat - 1 + is_top, (lon + is_top * (nlon // 2) + d + nlon) % nlon)

    def down(d):
        return (lat + 1 - is_bottom, (lon + is_bottom * (nlon // 2) + d + nlon) % nlon)

    barrier = pltpu.get_barrier_semaphore()
    partners = [west, east] + [up(d) for d in (-1, 0, 1)] + [down(d) for d in (-1, 0, 1)]
    for partner in partners:
        pl.semaphore_signal(barrier, inc=1, device_id=partner, device_id_type=pl.DeviceIdType.MESH)

    def body(i, _):
        for u in range(4):
            y = i * 4 + u
            v = x_ref[y, cols - tile :].astype(F32)
            for i_col in range(left):
                at = tile - left + i_col
                col_e[i_col, pl.ds(y, 1)] = v[at : at + 1]
            v = x_ref[y, :tile].astype(F32)
            for i_col in range(right):
                col_w[i_col, pl.ds(y, 1)] = v[i_col : i_col + 1]
        return 0

    lax.fori_loop(0, rows // 4, body, 0)
    send_e[...] = col_e[...].astype(BF16)
    send_w[...] = col_w[...].astype(BF16)
    pl.semaphore_wait(barrier, len(partners))

    copies = []

    def send(src, dst, slot, device):
        copy = pltpu.make_async_remote_copy(
            src_ref=src,
            dst_ref=dst,
            send_sem=send_sem.at[len(copies)],
            recv_sem=recv_sem.at[slot],
            device_id=device,
            device_id_type=pl.DeviceIdType.MESH,
        )
        copy.start()
        copies.append(copy)

    for place, y0, side in ((up, 0, 1 - is_top), (down, rows - above, is_bottom)):
        send(x_ref.at[pl.ds(y0, above)], lines.at[side], 2 + side * 3, place(0))
        send(x_ref.at[pl.ds(y0, above), pl.ds(cols - tile, tile)], corner_w.at[side], 3 + side * 3, place(1))
        send(x_ref.at[pl.ds(y0, above), pl.ds(0, tile)], corner_e.at[side], 4 + side * 3, place(-1))
    send(send_e, recv_w, 0, east)
    send(send_w, recv_e, 1, west)
    return copies


def exchange_wait(copies, recv_w, recv_e, lines, corner_w, corner_e, recv_sem):
    for slot, buffer in ((0, recv_w), (1, recv_e)):
        pltpu.make_async_copy(buffer, buffer, recv_sem.at[slot]).wait()
    for side in range(2):
        for k, buffer in enumerate((lines, corner_w, corner_e)):
            pltpu.make_async_copy(buffer.at[side], buffer.at[side], recv_sem.at[2 + side * 3 + k]).wait()
    for copy in copies:
        copy.wait_send()


def flip_lines(v, swap):
    pieces = [v[:, i : i + 128] for i in range(0, v.shape[1], 128)]
    half = len(pieces) // 2
    pieces = pieces[half:] + pieces[:half]
    if swap:
        pieces = [pltpu.roll(p, swap, 1) for p in pieces]
    return jnp.concatenate(pieces, axis=1)


def conv_kernel(
    left, right, above, below, groups, swap, taps,
    x_ref, w_ref, bias_ref, gain_ref, out_ref,
    xs, west_col, east_col, col_e, col_w, send_e, send_w, recv_w, recv_e, lines, corner_w, corner_e, send_sem, recv_sem,
):
    rows, cols, channels = x_ref.shape
    outs = w_ref.shape[1]
    tile = corner_w.shape[2]
    copies = exchange_start(
        left, right, x_ref, col_e, col_w, send_e, send_w, recv_w, recv_e, lines, corner_w, corner_e,
        (send_sem, recv_sem),
    )

    def shifted(y, line):
        xs[left, y] = line
        wide = line.astype(F32)
        for k in range(1, left + 1):
            xs[left - k, y] = pltpu.roll(wide, k, 0).astype(BF16)
        for k in range(1, right + 1):
            xs[left + k, y] = pltpu.roll(wide, cols - k, 0).astype(BF16)

    def fill(i, _):
        for u in range(2):
            y = i * 2 + u
            shifted(above + y, x_ref[y])
        return 0

    lax.fori_loop(0, rows // 2, fill, 0)
    exchange_wait(copies, recv_w, recv_e, lines, corner_w, corner_e, recv_sem)

    nlat = lax.axis_size("lat")
    lat = lax.axis_index("lat")

    def line(buffer, side, k):
        polar = lat == (0 if side == 0 else nlat - 1)
        plain = buffer[side, k].astype(F32)
        mirrored = flip_lines(buffer[side, above - 1 - k].astype(F32), swap)
        share = jnp.where(polar, 1.0, 0.0)
        return mirrored * share + plain * (1.0 - share)

    for i in range(left):
        west_col[i, pl.ds(0, rows)] = recv_w[i].astype(F32)
    for i in range(right):
        east_col[i, pl.ds(0, rows)] = recv_e[i].astype(F32)
    edge = rows
    for side, count, start in ((0, above, 0), (1, below, above + rows)):
        for k in range(count):
            shifted(start + k, line(lines, side, k).astype(BF16))
            corner = line(corner_w, side, k)
            for i in range(left):
                west_col[i, pl.ds(edge, 1)] = corner[tile - left + i : tile - left + i + 1]
            corner = line(corner_e, side, k)
            for i in range(right):
                east_col[i, pl.ds(edge, 1)] = corner[i : i + 1]
            edge += 1

    spot = lax.broadcasted_iota(jnp.int32, (tile, channels), 0)

    def patch(y, edge):
        for k in range(1, left + 1):
            v = xs[left - k, y, :tile].astype(F32)
            for i in range(k):
                v = jnp.where(spot == i, west_col[left - k + i, pl.ds(edge, 1)], v)
            xs[left - k, y, :tile] = v.astype(BF16)
        for k in range(1, right + 1):
            v = xs[left + k, y, cols - tile :].astype(F32)
            for i in range(k):
                v = jnp.where(spot == tile - k + i, east_col[i, pl.ds(edge, 1)], v)
            xs[left + k, y, cols - tile :] = v.astype(BF16)

    def patch_rows(i, _):
        for u in range(4):
            y = i * 4 + u
            patch(above + y, y)
        return 0

    lax.fori_loop(0, rows // 4, patch_rows, 0)
    for k in range(above):
        patch(k, rows + k)
    for k in range(below):
        patch(above + rows + k, rows + above + k)

    chunk = 8
    size = outs // groups
    if groups > 1:
        row = lax.broadcasted_iota(jnp.int32, (outs, outs), 0) // size
        col = lax.broadcasted_iota(jnp.int32, (outs, outs), 1) // size
        average = jnp.where(row == col, 1.0 / size, 0.0).astype(BF16)
    bias = jnp.concatenate([bias_ref[...]] * groups, axis=1)
    gain = jnp.concatenate([gain_ref[...]] * groups, axis=1)

    def body(i, _):
        y0 = i * chunk
        total = jnp.zeros((chunk * cols, outs), F32)
        at = 0
        for dy, row_taps in enumerate(taps):
            parts = []
            for dx, lanes in row_taps:
                parts.append(xs[dx, pl.ds(y0 + dy, chunk), :, lanes : lanes + 128].reshape(chunk * cols, 128))
            lhs = jnp.concatenate(parts, axis=1)
            depth = lhs.shape[1]
            total += jnp.dot(lhs, w_ref[at : at + depth], preferred_element_type=F32)
            at += depth
        total += bias
        square = total * total
        if groups > 1:
            high = square.astype(BF16)
            low = (square - high.astype(F32)).astype(BF16)
            mean = jnp.dot(high, average, preferred_element_type=F32) + jnp.dot(
                low, average, preferred_element_type=F32
            )
        else:
            mean = jnp.mean(square, axis=-1, keepdims=True)
        scaled = total * lax.rsqrt(mean + 1e-5) * gain
        out_ref[pl.ds(y0, chunk)] = gelu(scaled).astype(BF16).reshape(chunk, cols, outs)
        return 0

    lax.fori_loop(0, rows // chunk, body, 0)


def conv_block(x, weights, bias, gain, left, right, above, below, groups, swap, taps, collective_id, name):
    rows, cols, ch = x.shape
    outs = weights.shape[1]
    tile = 16
    extra = rows + 8
    vmem = pl.BlockSpec(memory_space=pltpu.VMEM)
    return pl.pallas_call(
        functools.partial(conv_kernel, left, right, above, below, groups, swap, taps),
        in_specs=[vmem] * 4,
        out_specs=vmem,
        out_shape=jax.ShapeDtypeStruct((rows, cols, outs), BF16),
        scratch_shapes=[
            pltpu.VMEM((left + right + 1, rows + above + below, cols, ch), BF16),
            pltpu.VMEM((left, extra, ch), F32),
            pltpu.VMEM((right, extra, ch), F32),
            pltpu.VMEM((left, rows, ch), F32),
            pltpu.VMEM((right, rows, ch), F32),
            pltpu.VMEM((left, rows, ch), BF16),
            pltpu.VMEM((right, rows, ch), BF16),
            pltpu.VMEM((left, rows, ch), BF16),
            pltpu.VMEM((right, rows, ch), BF16),
            pltpu.VMEM((2, above, cols, ch), BF16),
            pltpu.VMEM((2, above, tile, ch), BF16),
            pltpu.VMEM((2, above, tile, ch), BF16),
            pltpu.SemaphoreType.DMA((8,)),
            pltpu.SemaphoreType.DMA((8,)),
        ],
        compiler_params=pltpu.CompilerParams(
            collective_id=collective_id, has_side_effects=True, vmem_limit_bytes=VMEM_LIMIT
        ),
        name=name,
    )(x, weights, bias[None], gain[None])


def taps_one():
    return [
        [(dx, (ry2 * 2 + rx2) * 128) for dx in range(3) for ry2 in range(2) for rx2 in range(2)
         if not (dy == 2 and ry2) and not (dx == 2 and rx2)]
        for dy in range(3)
    ]


def taps_two():
    return [[(dx, lanes) for dx in range(4) for lanes in (0, 128)] for _ in range(4)]


def weights_one(kernel):
    _, _, ci, co = kernel.shape
    parts = []
    for sy in range(2):
        for sx in range(2):
            parts.append(jnp.pad(kernel, ((1 + 2 * sy, 4 - 2 * sy), (1 + 2 * sx, 4 - 2 * sx), (0, 0), (0, 0))))
    full = jnp.concatenate(parts, axis=-1)
    full = full.reshape(3, 2, 2, 3, 2, 2, ci, 4 * co).transpose(0, 3, 1, 4, 2, 5, 6, 7)
    full = full.reshape(9, 16 * ci, 4 * co)
    used = [full[dy * 3 + dx, lanes : lanes + 128] for dy, row in enumerate(taps_one()) for dx, lanes in row]
    return jnp.concatenate(used, axis=0)


def weights_two(kernel):
    _, _, ci, co = kernel.shape
    full = jnp.pad(kernel, ((1, 0), (1, 0), (0, 0), (0, 0)))
    return full.reshape(4, 2, 4, 2, ci, co).transpose(0, 2, 1, 3, 4, 5).reshape(16 * 4 * ci, co)


def local(
    cell_state,
    remap_weight,
    block_target,
    block_count,
    border_state,
    border_weight,
    border_target,
    kernel_one,
    bias_one,
    gain_one,
    kernel_two,
    bias_two,
    gain_two,
):
    patch_rows = TH // PH
    patch_cols = W // PW
    rim = EDGE * patch_rows
    nlon = lax.axis_size("lon")
    to_west, to_east = border_sums(border_state[0, 0], border_weight[0, 0], border_target[0, 0], 2 * rim)
    from_west = lax.ppermute(to_east, "lon", [(i, (i + 1) % nlon) for i in range(nlon)])
    from_east = lax.ppermute(to_west, "lon", [((i + 1) % nlon, i) for i in range(nlon)])
    acc = inner_sums(
        cell_state[0, 0], remap_weight[0, 0], block_target[0, 0], block_count[0], patch_rows * patch_cols
    )
    field = build_field(acc, from_west, from_east, patch_rows, patch_cols)
    one = weights_one(kernel_one)
    two = weights_two(kernel_two)
    ci = kernel_one.shape[2]
    hidden = conv_block(field, one, bias_one, gain_one, 1, 1, 1, 1, 4, 2 * ci, taps_one(), 0, "first")
    return conv_block(hidden, two, bias_two, gain_two, 2, 1, 2, 1, 1, 0, taps_two(), 1, "second")


def solution(mesh):
    placed = (
        P("lat", "lon", None, None, None),
        P("lat", "lon", None, None, None),
        P("lat", "lon", None),
        P("lat", "lon"),
        P("lat", "lon", None, None, None),
        P("lat", "lon", None, None, None),
        P("lat", "lon", None),
        P(),
        P(),
        P(),
        P(),
        P(),
        P(),
    )
    return jax.shard_map(
        local, mesh=mesh, in_specs=placed, out_specs=P("lat", "lon", None), check_vma=False
    )
```

profile of v0, /device:TPU:0, one launch (start us, length us, event | category | flops | bytes accessed | tf_op | source)
XLA Modules:
  0.0 84.8 jit_solution(5680759704472665037)
XLA Ops:
  0.0 0.0 copy-start.2
  0.0 8.8 %border_sums.1 = (bf16[32,32,128]{2,1,0:T(8,128)(2,1)}, bf16[32,32,128]{2,1,0:T(8,128)(2,1)}) custom-call(s32[128]{0:T(128)} %bitcast.159, bf16[32,64,128]{2,1,0:T(8,128)(2,1)} %bitcast.155, bf16[128,64,128]{2,1,0:T(8,128)(2,1)} %bitcast.154), custom_call_target="tpu_custom_call" | custom-call | tf_op jit(solution)/shard_map/border_sums/pallas_call | solution.py:97
  8.8 3.0 %collective-permute-start = (bf16[32,32,128]{2,1,0:T(8,128)(2,1)}, bf16[32,32,128]{2,1,0:T(8,128)(2,1)S(1)}, u32[]{:S(2)}, u32[]{:S(2)}) collective-permute-start(bf16[32,32,128]{2,1,0:T(8,128)(2,1)} %get-tuple-element.7), channel_id=1, source_target_pairs={{0,1},{1,2},{2,3},{3,4},{4,5},{5,6},{6,7},{7,0},{8,9},{9,10},{10,1... | collective-permute-start | bytes 786440 | tf_op jit(solution)/shard_map/ppermute | solution.py:524
  11.8 3.0 %collective-permute-start.1 = (bf16[32,32,128]{2,1,0:T(8,128)(2,1)}, bf16[32,32,128]{2,1,0:T(8,128)(2,1)S(1)}, u32[]{:S(2)}, u32[]{:S(2)}) collective-permute-start(bf16[32,32,128]{2,1,0:T(8,128)(2,1)} %get-tuple-element.8), channel_id=1, source_target_pairs={{1,0},{2,1},{3,2},{4,3},{5,4},{6,5},{7,6},{0,7},{9,8},{10,9},{11,1... | collective-permute-start | bytes 786440 | tf_op jit(solution)/shard_map/ppermute | solution.py:525
  14.9 0.0 copy-done.2
  14.9 0.8 fusion.7
  15.7 0.3 copy.15
  16.0 0.0 copy-start.1
  17.0 0.1 copy-done.1
  17.1 0.1 pad.24
  17.3 1.2 %copy.16 = bf16[4,2,4,2,64,128]{5,4,3,1,2,0:T(8,128)(2,1)} copy(bf16[4,2,4,2,64,128]{5,4,3,2,1,0:T(8,128)(2,1)S(1)} %bitcast.152) | data formatting | bytes 2097152 | tf_op jit(solution)/shard_map/reshape | solution.py:501
  18.4 11.2 %inner_sums.1.acc_ref = f32[256,32,128]{2,1,0:T(8,128)} custom-call(s32[512]{0:T(512)} %bitcast.156, s32[1]{0:T(128)} %bitcast.123.live_ref, bf16[32,64,512]{2,1,0:T(8,128)(2,1)} %bitcast.153, bf16[512,64,128]{2,1,0:T(8,128)(2,1)} %bitcast.125), custom_call_target="tpu_custom_call" | custom-call | tf_op jit(solution)/shard_map/inner_sums/pallas_call | solution.py:139
  29.7 0.0 copy-start
  29.7 0.0 collective-permute-done.west_ref
  29.7 0.0 copy-start.3
  29.7 0.0 collective-permute-done.1.east_ref
  29.7 0.7 copy-done.3
  30.4 0.0 copy-start.4
  30.5 0.7 copy-done.4
  31.2 7.7 %field.1.x_ref = bf16[64,32,512]{2,1,0:T(8,128)(2,1)} custom-call(f32[256,32,128]{2,1,0:T(8,128)} %inner_sums.1.acc_ref, bf16[32,32,128]{2,1,0:T(8,128)(2,1)} %copy-done.3, bf16[32,32,128]{2,1,0:T(8,128)(2,1)} %copy-done.4, bf16[512,512]{1,0:T(8,128)(2,1)} %constant.5.clone.place_ref), custom_call_target="tpu_custom_call" | custom-call | tf_op jit(solution)/shard_map/field/pallas_call | solution.py:208
  38.8 0.0 copy-done
  38.8 25.9 %first.1.x_ref = bf16[64,32,256]{2,1,0:T(8,128)(2,1)} custom-call(bf16[64,32,512]{2,1,0:T(8,128)(2,1)} %field.1.x_ref, bf16[3200,256]{1,0:T(8,128)(2,1)} %copy-done, f32[1,64]{1,0:T(1,128)} %bitcast.160, f32[1,64]{1,0:T(1,128)} %bitcast.161), custom_call_target="tpu_custom_call" | custom-call | tf_op jit(solution)/shard_map/first/pallas_call | solution.py:445
  64.8 18.2 %second.1 = bf16[64,32,128]{2,1,0:T(8,128)(2,1)} custom-call(bf16[64,32,256]{2,1,0:T(8,128)(2,1)} %first.1.x_ref, bf16[4096,128]{1,0:T(8,128)(2,1)} %bitcast.151, f32[1,128]{1,0:T(1,128)} %bitcast.157, f32[1,128]{1,0:T(1,128)} %bitcast.158), custom_call_target="tpu_custom_call" | custom-call | tf_op jit(solution)/shard_map/second/pallas_call | solution.py:445
  82.9 1.9 %copy.43 = bf16[64,32,128]{2,1,0:T(8,128)(2,1)} copy(bf16[64,32,128]{2,1,0:T(8,128)(2,1)} %second.1) | data formatting | bytes 1048576
  (25 shorter events, 0.2 us)
Async XLA Ops:
  0.0 14.9 %copy-start.2 = (bf16[7,7,32,64]{3,2,1,0:T(8,128)(2,1)S(1)}, bf16[7,7,32,64]{3,2,1,0:T(8,128)(2,1)}, u32[]{:S(2)}) copy-start(bf16[7,7,32,64]{3,2,1,0:T(8,128)(2,1)} %param.21) | copy-start | bytes 602116
  8.8 20.8 %collective-permute-start = (bf16[32,32,128]{2,1,0:T(8,128)(2,1)}, bf16[32,32,128]{2,1,0:T(8,128)(2,1)S(1)}, u32[]{:S(2)}, u32[]{:S(2)}) collective-permute-start(bf16[32,32,128]{2,1,0:T(8,128)(2,1)} %get-tuple-element.7), channel_id=1, source_target_pairs={{0,1},{1,2},{2,3},{3,4},{4,5},{5,6},{6,7},{7,0},{8,9},{9,10},{10,1... | collective-permute-start | bytes 786440 | tf_op jit(solution)/shard_map/ppermute | solution.py:524
  11.8 17.9 %collective-permute-start.1 = (bf16[32,32,128]{2,1,0:T(8,128)(2,1)}, bf16[32,32,128]{2,1,0:T(8,128)(2,1)S(1)}, u32[]{:S(2)}, u32[]{:S(2)}) collective-permute-start(bf16[32,32,128]{2,1,0:T(8,128)(2,1)} %get-tuple-element.8), channel_id=1, source_target_pairs={{1,0},{2,1},{3,2},{4,3},{5,4},{6,5},{7,6},{0,7},{9,8},{10,9},{11,1... | collective-permute-start | bytes 786440 | tf_op jit(solution)/shard_map/ppermute | solution.py:525
  16.0 1.1 %copy-start.1 = (bf16[7,7,64,128]{3,2,1,0:T(8,128)(2,1)S(1)}, bf16[7,7,64,128]{3,2,1,0:T(8,128)(2,1)}, u32[]{:S(2)}) copy-start(bf16[7,7,64,128]{3,2,1,0:T(8,128)(2,1)} %param.24) | copy-start | bytes 2408452
  29.7 9.1 %copy-start = (bf16[3200,256]{1,0:T(8,128)(2,1)}, bf16[3200,256]{1,0:T(8,128)(2,1)S(1)}, u32[]{:S(2)}) copy-start(bf16[3200,256]{1,0:T(8,128)(2,1)S(1)} %fusion.9.w_ref) | copy-start | bytes 4915204
  29.7 0.8 copy-start.3
  30.4 0.7 copy-start.4
where the time goes:
time: 85.5 us; the launch traced here: 84.8 us
  Pallas kernels  71.9 us (84%)
  starting transfers between devices  6.01 us (7%)
  local copies, waits for them, and re-layouts  5.21 us (6%)
  between operations  0.92 us (1%)
    pallas_call x2, Pallas kernels, conv_block(): pl.pallas_call(functools.partial(conv_kernel, left, right, above, below,...  44.1 us
    pallas_call x1, Pallas kernels, inner_sums(): pl.pallas_call(functools.partial(inner_kernel, patches // block), grid_sp...  11.2 us
    pallas_call x1, Pallas kernels, border_sums(): pl.pallas_call(border_kernel, grid_spec=pltpu.PrefetchScalarGridSpec(num_...  8.85 us
    pallas_call x1, Pallas kernels, build_field(): pl.pallas_call(functools.partial(field_kernel, patch_cols), grid=(patch_r...  7.66 us
    unnamed x35, local copies, waits for them, and re-layouts  3.62 us
    ppermute x1, starting transfers between devices, local(): lax.ppermute(to_west, 'lon', [((i + 1) % nlon, i) for i in range(nlon)])  3.04 us
    ppermute x1, starting transfers between devices, local(): lax.ppermute(to_east, 'lon', [(i, (i + 1) % nlon) for i in range(nlon)])  2.98 us
  transfers between devices with their start and end apart: 2, of which 0 were waited for; matrix products, arithmetic and copies ran while one was open for 3% of the time, Pallas kernels for 13%

commit v1 on v0

--- a/solution.py
+++ b/solution.py
@@ -14,7 +14,7 @@
 TH = 256
 W = 128
 PACK = 4
-VMEM_LIMIT = 56 * 1024 * 1024
+VMEM_LIMIT = 32 * 1024 * 1024
 F32 = jnp.float32
 BF16 = jnp.bfloat16
 
@@ -35,8 +35,7 @@
             else:
                 other = pltpu.roll(v.astype(F32), block - distance, 1).astype(BF16)
                 pair = jnp.concatenate([v, other], axis=0)
-            pair = pair.T.astype(F32)
-            turned[pl.ds(c, pair.shape[0], stride=channels)] = pair
+            turned[pl.ds(c, distance, stride=channels)] = pair.T[:distance].astype(F32)
         return 0
 
     lax.fori_loop(0, channels // 2, body, 0)
@@ -69,10 +68,9 @@
     mask = slot_mask(channels, cells)
 
     def body(i, _):
-        for u in range(4):
-            g = i * 4 + u
-            prod = group_product(turned, w_ref, mask, g, channels, distance)
-            for k, slot in enumerate(group_slots(g, distance)):
+        prods = [group_product(turned, w_ref, mask, i * 4 + u, channels, distance) for u in range(4)]
+        for u, prod in enumerate(prods):
+            for k, slot in enumerate(group_slots(i * 4 + u, distance)):
                 store(base + slot, prod[k * channels : (k + 1) * channels])
         return 0
 
@@ -104,7 +102,7 @@
                 pl.BlockSpec((n, b, pixels), lambda i, t: (0, 0, 0)),
             ],
             out_specs=[pl.BlockSpec((count // 2, c, pixels), lambda i, t: (0, 0, 0))] * 2,
-            scratch_shapes=[pltpu.VMEM((count, c, pixels), F32), pltpu.VMEM((n * c, 2 * b), F32)],
+            scratch_shapes=[pltpu.VMEM((count, c, pixels), F32), pltpu.VMEM((n // 2 * c, 2 * b), F32)],
         ),
         out_shape=[jax.ShapeDtypeStruct((count // 2, c, pixels), BF16)] * 2,
         compiler_params=params(),
@@ -165,21 +163,21 @@
     return table
 
 
-def field_kernel(cols, acc_ref, west_ref, east_ref, place_ref, out_ref):
-    prows = out_ref.shape[0] // (PH // 4)
+def field_step(step, prows, cols, acc_ref, west_ref, east_ref, place_ref, out_ref):
     channels = acc_ref.shape[1]
     wide = PACK * (PW // 4)
     rows = []
     for r in range(prows):
+        prow = step * prows + r
         for jg in range(cols // PACK):
             parts = []
             for j in range(PACK):
                 col = jg * PACK + j
-                v = acc_ref[r * cols + col]
+                v = acc_ref[prow * cols + col]
                 if col == 0:
-                    v = v + west_ref[r].astype(F32)
+                    v = v + west_ref[prow].astype(F32)
                 if col == cols - 1:
-                    v = v + east_ref[r].astype(F32)
+                    v = v + east_ref[prow].astype(F32)
                 parts.append(v.astype(BF16))
             rows.append(jnp.concatenate(parts, axis=1))
     moved = jnp.dot(jnp.concatenate(rows, axis=0), place_ref[...], preferred_element_type=F32)
@@ -196,38 +194,10 @@
                     start = (rx2 * (PH // 2) + py) * wide
                     lane = ((py % 2) * 2 + rx2) * 4 * channels
                     out_ref[
-                        r * (PH // 4) + py // 2, jg * wide : (jg + 1) * wide, lane : lane + 4 * channels
+                        (step * prows + r) * (PH // 4) + py // 2,
+                        jg * wide : (jg + 1) * wide,
+                        lane : lane + 4 * channels,
                     ] = turned[start : start + wide]
-
-
-def build_field(acc, west, east, patch_rows, patch_cols):
-    _, c, pixels = acc.shape
-    step = 4
-    per = step * PH // 4
-    place = jnp.asarray(placement(), BF16)
-    return pl.pallas_call(
-        functools.partial(field_kernel, patch_cols),
-        grid=(patch_rows // step,),
-        in_specs=[
-            pl.BlockSpec((step * patch_cols, c, pixels), lambda i: (i, 0, 0)),
-            pl.BlockSpec((step, c, pixels), lambda i: (i, 0, 0)),
-            pl.BlockSpec((step, c, pixels), lambda i: (i, 0, 0)),
-            pl.BlockSpec(place.shape, lambda i: (0, 0)),
-        ],
-        out_specs=pl.BlockSpec((per, patch_cols * PW // 4, 16 * c), lambda i: (i, 0, 0)),
-        out_shape=jax.ShapeDtypeStruct((patch_rows * PH // 4, patch_cols * PW // 4, 16 * c), BF16),
-        compiler_params=params(),
-        name="field",
-    )(acc, west, east, place)
-
-
-def flip_lines(v, swap):
-    pieces = [v[:, i : i + 128] for i in range(0, v.shape[1], 128)]
-    half = len(pieces) // 2
-    pieces = pieces[half:] + pieces[:half]
-    if swap:
-        pieces = [pltpu.roll(p, swap, 1) for p in pieces]
-    return jnp.concatenate(pieces, axis=1)
 
 
 def gelu(v):
@@ -235,27 +205,37 @@
     return 0.5 * v * (1.0 + jnp.tanh(inner))
 
 
-def exchange_start(left, right, x_ref, col_e, col_w, send_e, send_w, recv_w, recv_e, lines, corner_w, corner_e, sems):
+def positions():
     nlat, nlon = lax.axis_size("lat"), lax.axis_size("lon")
+    lat, lon = lax.axis_index("lat"), lax.axis_index("lon")
+    is_top, is_bottom = (nlat - lat) // nlat, (lat + 1) // nlat
+    west = (lat, (lon + nlon - 1) % nlon)
+    east = (lat, (lon + 1) % nlon)
+
+    def up(d):
+        return (lat - 1 + is_top, (lon + is_top * (nlon // 2) + d + nlon) % nlon)
+
+    def down(d):
+        return (lat + 1 - is_bottom, (lon + is_bottom * (nlon // 2) + d + nlon) % nlon)
+
+    return is_top, is_bottom, west, east, up, down
+
+
+def greet():
+    _, _, west, east, up, down = positions()
+    partners = [west, east] + [up(d) for d in (-1, 0, 1)] + [down(d) for d in (-1, 0, 1)]
+    barrier = pltpu.get_barrier_semaphore()
+    for partner in partners:
+        pl.semaphore_signal(barrier, inc=1, device_id=partner, device_id_type=pl.DeviceIdType.MESH)
+    return barrier, len(partners)
+
+
+def exchange_start(left, right, greeted, x_ref, col_e, col_w, send_e, send_w, recv_w, recv_e, lines, corner_w, corner_e, sems):
     rows, cols, _ = x_ref.shape
     above = lines.shape[1]
     tile = corner_w.shape[2]
     send_sem, recv_sem = sems
-    lat, lon = lax.axis_index("lat"), lax.axis_index("lon")
-    is_top, is_bottom = (nlat - lat) // nlat, (lat + 1) // nlat
-    west = (lat, (lon + nlon - 1) % nlon)
-    east = (lat, (lon + 1) % nlon)
-
-    def up(d):
-        return (lat - 1 + is_top, (lon + is_top * (nlon // 2) + d + nlon) % nlon)
-
-    def down(d):
-        return (lat + 1 - is_bottom, (lon + is_bottom * (nlon // 2) + d + nlon) % nlon)
-
-    barrier = pltpu.get_barrier_semaphore()
-    partners = [west, east] + [up(d) for d in (-1, 0, 1)] + [down(d) for d in (-1, 0, 1)]
-    for partner in partners:
-        pl.semaphore_signal(barrier, inc=1, device_id=partner, device_id_type=pl.DeviceIdType.MESH)
+    is_top, is_bottom, west, east, up, down = positions()
 
     def body(i, _):
         for u in range(4):
@@ -272,7 +252,8 @@
     lax.fori_loop(0, rows // 4, body, 0)
     send_e[...] = col_e[...].astype(BF16)
     send_w[...] = col_w[...].astype(BF16)
-    pl.semaphore_wait(barrier, len(partners))
+    if greeted is not None:
+        pl.semaphore_wait(*greeted)
 
     copies = []
 
@@ -316,8 +297,8 @@
     return jnp.concatenate(pieces, axis=1)
 
 
-def conv_kernel(
-    left, right, above, below, groups, swap, taps,
+def conv_layer(
+    left, right, above, below, groups, swap, taps, greeted,
     x_ref, w_ref, bias_ref, gain_ref, out_ref,
     xs, west_col, east_col, col_e, col_w, send_e, send_w, recv_w, recv_e, lines, corner_w, corner_e, send_sem, recv_sem,
 ):
@@ -325,7 +306,7 @@
     outs = w_ref.shape[1]
     tile = corner_w.shape[2]
     copies = exchange_start(
-        left, right, x_ref, col_e, col_w, send_e, send_w, recv_w, recv_e, lines, corner_w, corner_e,
+        left, right, greeted, x_ref, col_e, col_w, send_e, send_w, recv_w, recv_e, lines, corner_w, corner_e,
         (send_sem, recv_sem),
     )
 
@@ -436,38 +417,73 @@
     lax.fori_loop(0, rows // chunk, body, 0)
 
 
-def conv_block(x, weights, bias, gain, left, right, above, below, groups, swap, taps, collective_id, name):
-    rows, cols, ch = x.shape
-    outs = weights.shape[1]
+def layer_scratch(left, right, above, below, rows, cols, ch):
     tile = 16
-    extra = rows + 8
+    return [
+        pltpu.VMEM((left + right + 1, rows + above + below, cols, ch), BF16),
+        pltpu.VMEM((left, rows + 8, ch), F32),
+        pltpu.VMEM((right, rows + 8, ch), F32),
+        pltpu.VMEM((left, rows, ch), F32),
+        pltpu.VMEM((right, rows, ch), F32),
+        pltpu.VMEM((left, rows, ch), BF16),
+        pltpu.VMEM((right, rows, ch), BF16),
+        pltpu.VMEM((left, rows, ch), BF16),
+        pltpu.VMEM((right, rows, ch), BF16),
+        pltpu.VMEM((2, above, cols, ch), BF16),
+        pltpu.VMEM((2, above, tile, ch), BF16),
+        pltpu.VMEM((2, above, tile, ch), BF16),
+        pltpu.SemaphoreType.DMA((8,)),
+        pltpu.SemaphoreType.DMA((8,)),
+    ]
+
+
+def encoder_kernel(
+    patch_cols, ci,
+    acc_ref, west_ref, east_ref, place_ref, w1_ref, bias1_ref, gain1_ref, w2_ref, bias2_ref, gain2_ref,
+    out_ref, field, hidden, *scratch,
+):
+    greeted = greet()
+    prows = 4
+    patch_rows = west_ref.shape[0]
+
+    def body(i, _):
+        field_step(i, prows, patch_cols, acc_ref, west_ref, east_ref, place_ref, field)
+        return 0
+
+    lax.fori_loop(0, patch_rows // prows, body, 0)
+    half = len(scratch) // 2
+    conv_layer(
+        1, 1, 1, 1, 4, 2 * ci, taps_one(), greeted,
+        field, w1_ref, bias1_ref, gain1_ref, hidden, *scratch[:half],
+    )
+    conv_layer(
+        2, 1, 2, 1, 1, 0, taps_two(), None,
+        hidden, w2_ref, bias2_ref, gain2_ref, out_ref, *scratch[half:],
+    )
+
+
+def encode(acc, west, east, patch_rows, patch_cols, one, bias_one, gain_one, two, bias_two, gain_two):
+    ci = acc.shape[1]
+    rows, cols = patch_rows * PH // 4, patch_cols * PW // 4
+    ch_one, ch_two, outs = 16 * ci, one.shape[1], two.shape[1]
     vmem = pl.BlockSpec(memory_space=pltpu.VMEM)
+    place = jnp.asarray(placement(), BF16)
     return pl.pallas_call(
-        functools.partial(conv_kernel, left, right, above, below, groups, swap, taps),
-        in_specs=[vmem] * 4,
+        functools.partial(encoder_kernel, patch_cols, ci),
+        in_specs=[vmem] * 10,
         out_specs=vmem,
         out_shape=jax.ShapeDtypeStruct((rows, cols, outs), BF16),
         scratch_shapes=[
-            pltpu.VMEM((left + right + 1, rows + above + below, cols, ch), BF16),
-            pltpu.VMEM((left, extra, ch), F32),
-            pltpu.VMEM((right, extra, ch), F32),
-            pltpu.VMEM((left, rows, ch), F32),
-            pltpu.VMEM((right, rows, ch), F32),
-            pltpu.VMEM((left, rows, ch), BF16),
-            pltpu.VMEM((right, rows, ch), BF16),
-            pltpu.VMEM((left, rows, ch), BF16),
-            pltpu.VMEM((right, rows, ch), BF16),
-            pltpu.VMEM((2, above, cols, ch), BF16),
-            pltpu.VMEM((2, above, tile, ch), BF16),
-            pltpu.VMEM((2, above, tile, ch), BF16),
-            pltpu.SemaphoreType.DMA((8,)),
-            pltpu.SemaphoreType.DMA((8,)),
+            pltpu.VMEM((rows, cols, ch_one), BF16),
+            pltpu.VMEM((rows, cols, ch_two), BF16),
+            *layer_scratch(1, 1, 1, 1, rows, cols, ch_one),
+            *layer_scratch(2, 1, 2, 1, rows, cols, ch_two),
         ],
         compiler_params=pltpu.CompilerParams(
-            collective_id=collective_id, has_side_effects=True, vmem_limit_bytes=VMEM_LIMIT
+            collective_id=0, has_side_effects=True, vmem_limit_bytes=VMEM_LIMIT
         ),
-        name=name,
-    )(x, weights, bias[None], gain[None])
+        name="encoder",
+    )(acc, west, east, place, one, bias_one[None], gain_one[None], two, bias_two[None], gain_two[None])
 
 
 def taps_one():
@@ -526,12 +542,11 @@
     acc = inner_sums(
         cell_state[0, 0], remap_weight[0, 0], block_target[0, 0], block_count[0], patch_rows * patch_cols
     )
-    field = build_field(acc, from_west, from_east, patch_rows, patch_cols)
     one = weights_one(kernel_one)
     two = weights_two(kernel_two)
-    ci = kernel_one.shape[2]
-    hidden = conv_block(field, one, bias_one, gain_one, 1, 1, 1, 1, 4, 2 * ci, taps_one(), 0, "first")
-    return conv_block(hidden, two, bias_two, gain_two, 2, 1, 2, 1, 1, 0, taps_two(), 1, "second")
+    return encode(
+        acc, from_west, from_east, patch_rows, patch_cols, one, bias_one, gain_one, two, bias_two, gain_two
+    )
 
 
 def solution(mesh):

time: 85.5 us -> 65 us (0.76)
  Pallas kernels: 71.9 us -> 48.9 us
  other arithmetic: 0.81 us -> 2.08 us
  local copies, waits for them, and re-layouts: 5.21 us -> 6.44 us
    pallas_call x3 -> x1, Pallas kernels: 51.8 us -> 30.4 us  [encode(): pl.pallas_call(functools.partial(encoder_kernel, patch_cols, ci), in_spec...]
    pallas_call x1, Pallas kernels: 8.85 us -> 5.26 us  [border_sums(): pl.pallas_call(border_kernel, grid_spec=pltpu.PrefetchScalarGridSpec(num_...]
    unnamed x35 -> x51, local copies, waits for them, and re-layouts: 3.62 us -> 5.96 us
    pallas_call x1, Pallas kernels: 11.2 us -> 13.3 us  [inner_sums(): pl.pallas_call(functools.partial(inner_kernel, patches // block), grid_sp...]
    concatenate x1, other arithmetic: 0.81 us -> 2.08 us  [weights_one(): full = jnp.concatenate(parts, axis=-1)]
    reshape x1, local copies, waits for them, and re-layouts: 1.16 us -> 0.11 us  [weights_two(): full.reshape(4, 2, 4, 2, ci, co).transpose(0, 2, 1, 3, 4, 5)]
  transfers between devices with their start and end apart: 2 -> 2, of which waited for: 0 -> 0; matrix products, arithmetic and copies ran while one was open for 3% -> 4% of each run, Pallas kernels for 13% -> 21%
where the time goes in v1:
time: 65 us; the launch traced here: 64.7 us
  Pallas kernels  48.9 us (75%)
  local copies, waits for them, and re-layouts  6.44 us (10%)
  starting transfers between devices  6.12 us (9%)
  other arithmetic  2.08 us (3%)
  between operations  1.16 us (2%)
    pallas_call x1, Pallas kernels, encode(): pl.pallas_call(functools.partial(encoder_kernel, patch_cols, ci), in_spec...  30.4 us
    pallas_call x1, Pallas kernels, inner_sums(): pl.pallas_call(functools.partial(inner_kernel, patches // block), grid_sp...  13.3 us
    unnamed x51, local copies, waits for them, and re-layouts  5.96 us
    pallas_call x1, Pallas kernels, border_sums(): pl.pallas_call(border_kernel, grid_spec=pltpu.PrefetchScalarGridSpec(num_...  5.26 us
    ppermute x1, starting transfers between devices, local(): lax.ppermute(to_west, 'lon', [((i + 1) % nlon, i) for i in range(nlon)])  3.11 us
    ppermute x1, starting transfers between devices, local(): lax.ppermute(to_east, 'lon', [(i, (i + 1) % nlon) for i in range(nlon)])  3.01 us
    concatenate x1, other arithmetic, weights_one(): full = jnp.concatenate(parts, axis=-1)  2.08 us
  transfers between devices with their start and end apart: 2, of which 0 were waited for; matrix products, arithmetic and copies ran while one was open for 4% of the time, Pallas kernels for 21%

profile of v1, /device:TPU:0, one launch (start us, length us, event | category | flops | bytes accessed | tf_op | source)
XLA Modules:
  0.0 64.7 jit_solution(5172498125198056751)
XLA Ops:
  0.0 0.0 copy-start.1
  0.0 1.6 %copy-done.1 = bf16[1,1,128,64,128]{4,3,2,1,0:T(8,128)(2,1)S(1)} copy-done((bf16[1,1,128,64,128]{4,3,2,1,0:T(8,128)(2,1)S(1)}, bf16[1,1,128,64,128]{4,3,2,1,0:T(8,128)(2,1)}, u32[]{:S(2)}) %copy-start.1) | copy-done | bytes 2097176
  1.6 0.0 copy-start.3
  1.6 1.0 %copy-done.3 = bf16[1,1,128,32,64]{2,4,3,1,0:T(8,128)(2,1)S(1)} copy-done((bf16[1,1,128,32,64]{2,4,3,1,0:T(8,128)(2,1)S(1)}, bf16[1,1,128,32,64]{2,4,3,1,0:T(8,128)(2,1)}, u32[]{:S(2)}) %copy-start.3) | copy-done | bytes 524312
  2.6 0.0 copy-start.9
  2.6 0.7 %copy-done.9 = s32[1,1,128]{2,1,0:T(1,128)S(1)} copy-done((s32[1,1,128]{2,1,0:T(1,128)S(1)}, s32[1,1,128]{2,1,0:T(1,128)}, u32[]{:S(2)}) %copy-start.9) | copy-done | bytes 536
  3.3 0.0 slice-start
  3.3 5.3 %border_sums.1 = (bf16[32,32,128]{2,1,0:T(8,128)(2,1)S(1)}, bf16[32,32,128]{2,1,0:T(8,128)(2,1)S(1)}) custom-call(s32[128]{0:T(128)S(1)} %bitcast.136, bf16[32,64,128]{2,1,0:T(8,128)(2,1)S(1)} %bitcast.130, bf16[128,64,128]{2,1,0:T(8,128)(2,1)S(1)} %bitcast.129), custom_call_target="tpu_custom_call" | custom-call | tf_op jit(solution)/shard_map/border_sums/pallas_call | solution.py:95
  8.6 3.0 %collective-permute-start = (bf16[32,32,128]{2,1,0:T(8,128)(2,1)S(1)}, bf16[32,32,128]{2,1,0:T(8,128)(2,1)S(1)}, u32[]{:S(2)}, u32[]{:S(2)}) collective-permute-start(bf16[32,32,128]{2,1,0:T(8,128)(2,1)S(1)} %get-tuple-element.7), channel_id=1, source_target_pairs={{0,1},{1,2},{2,3},{3,4},{4,5},{5,6},{6,7},{7,0},{8,9},{9,10},{10,1... | collective-permute-start | bytes 786440 | tf_op jit(solution)/shard_map/ppermute | solution.py:540
  11.6 3.1 %collective-permute-start.1 = (bf16[32,32,128]{2,1,0:T(8,128)(2,1)S(1)}, bf16[32,32,128]{2,1,0:T(8,128)(2,1)S(1)}, u32[]{:S(2)}, u32[]{:S(2)}) collective-permute-start(bf16[32,32,128]{2,1,0:T(8,128)(2,1)S(1)} %get-tuple-element.8), channel_id=1, source_target_pairs={{1,0},{2,1},{3,2},{4,3},{5,4},{6,5},{7,6},{0,7},{9,8},{10,9},{11,1... | collective-permute-start | bytes 786440 | tf_op jit(solution)/shard_map/ppermute | solution.py:541
  14.7 2.1 %fusion.7 = bf16[12,12,32,256]{3,2,1,0:T(8,128)(2,1)S(1)} fusion(bf16[7,7,32,64]{3,2,1,0:T(8,128)(2,1)} %param.21), kind=kLoop, calls=%fused_computation.13 | loop fusion | flops 23592960 | bytes 2560000 | tf_op jit(solution)/shard_map/concatenate | solution.py:507
  16.8 0.0 slice-start.1
  16.8 0.2 copy.15
  17.0 0.0 copy-start.10
  18.2 0.1 copy-done.10
  18.3 0.0 copy-start
  18.3 0.0 copy-start.4
  18.3 0.1 pad.24
  18.5 0.1 copy.16
  18.6 0.0 slice-done
  18.6 0.6 slice-done.1
  19.2 0.9 %copy-done = bf16[1,1,512,32,64]{2,4,3,1,0:T(8,128)(2,1)S(1)} copy-done((bf16[1,1,512,32,64]{2,4,3,1,0:T(8,128)(2,1)S(1)}, bf16[1,1,512,32,64]{2,4,3,1,0:T(8,128)(2,1)}, u32[]{:S(2)}) %copy-start) | copy-done | bytes 2097176
  20.1 0.0 copy-done.4
  20.1 0.0 copy-start.2
  20.1 0.0 copy-start.5
  20.1 0.0 copy-start.6
  20.1 0.0 copy-start.7
  20.2 0.0 copy-start.8
  20.2 13.3 %inner_sums.1.acc_ref = f32[256,32,128]{2,1,0:T(8,128)S(1)} custom-call(s32[512]{0:T(512)S(1)} %bitcast.131, s32[1]{0:T(128)} %bitcast.123.live_ref, bf16[32,64,512]{2,1,0:T(8,128)(2,1)S(1)} %bitcast.128, bf16[512,64,128]{2,1,0:T(8,128)(2,1)S(1)} %bitcast.126), custom_call_target="tpu_custom_call" | custom-call | tf_op jit(solution)/shard_map/inner_sums/pallas_call | solution.py:137
  33.5 0.0 collective-permute-done.west_ref
  33.5 0.0 collective-permute-done.1.east_ref
  33.5 0.0 copy-done.2
  33.5 0.0 copy-done.5
  33.5 0.0 copy-done.6
  33.5 0.0 copy-done.7
  33.6 0.0 copy-done.8
  33.6 30.4 %encoder.1 = bf16[64,32,128]{2,1,0:T(8,128)(2,1)S(1)} custom-call(f32[256,32,128]{2,1,0:T(8,128)S(1)} %inner_sums.1.acc_ref, bf16[32,32,128]{2,1,0:T(8,128)(2,1)S(1)} %collective-permute-done.west_ref, bf16[32,32,128]{2,1,0:T(8,128)(2,1)S(1)} %collective-permute-done.1.east_ref, bf16[512,512]{1,0:T(8,128)(2,1)S(1)} %copy-done.2, ...), custom_call_target="tpu_custom_call" | custom-call | tf_op jit(solution)/shard_map/encoder/pallas_call | solution.py:471
  63.9 0.8 %copy.43 = bf16[64,32,128]{2,1,0:T(8,128)(2,1)} copy(bf16[64,32,128]{2,1,0:T(8,128)(2,1)S(1)} %encoder.1) | data formatting | bytes 1048576
  (26 shorter events, 0.2 us)
Async XLA Ops:
  0.0 1.6 %copy-start.1 = (bf16[1,1,128,64,128]{4,3,2,1,0:T(8,128)(2,1)S(1)}, bf16[1,1,128,64,128]{4,3,2,1,0:T(8,128)(2,1)}, u32[]{:S(2)}) copy-start(bf16[1,1,128,64,128]{4,3,2,1,0:T(8,128)(2,1)} %param.19) | copy-start | bytes 6291460
  1.6 1.0 %copy-start.3 = (bf16[1,1,128,32,64]{2,4,3,1,0:T(8,128)(2,1)S(1)}, bf16[1,1,128,32,64]{2,4,3,1,0:T(8,128)(2,1)}, u32[]{:S(2)}) copy-start(bf16[1,1,128,32,64]{2,4,3,1,0:T(8,128)(2,1)} %param.18) | copy-start | bytes 1572868
  2.6 0.7 %copy-start.9 = (s32[1,1,128]{2,1,0:T(1,128)S(1)}, s32[1,1,128]{2,1,0:T(1,128)}, u32[]{:S(2)}) copy-start(s32[1,1,128]{2,1,0:T(1,128)} %param.20) | copy-start | bytes 1540
  3.3 15.3 %slice-start = ((s8[8388608]{0:T(1024)(128)(4,1)}), s8[4194304]{0:T(1024)(128)(4,1)S(1)}, s32[]{:S(2)}) async-start(s8[8388608]{0:T(1024)(128)(4,1)} %bitcast.124), calls=%async_computation | async-start | bytes 8388608
  8.6 24.9 %collective-permute-start = (bf16[32,32,128]{2,1,0:T(8,128)(2,1)S(1)}, bf16[32,32,128]{2,1,0:T(8,128)(2,1)S(1)}, u32[]{:S(2)}, u32[]{:S(2)}) collective-permute-start(bf16[32,32,128]{2,1,0:T(8,128)(2,1)S(1)} %get-tuple-element.7), channel_id=1, source_target_pairs={{0,1},{1,2},{2,3},{3,4},{4,5},{5,6},{6,7},{7,0},{8,9},{9,10},{10,1... | collective-permute-start | bytes 786440 | tf_op jit(solution)/shard_map/ppermute | solution.py:540
  11.6 21.9 %collective-permute-start.1 = (bf16[32,32,128]{2,1,0:T(8,128)(2,1)S(1)}, bf16[32,32,128]{2,1,0:T(8,128)(2,1)S(1)}, u32[]{:S(2)}, u32[]{:S(2)}) collective-permute-start(bf16[32,32,128]{2,1,0:T(8,128)(2,1)S(1)} %get-tuple-element.8), channel_id=1, source_target_pairs={{1,0},{2,1},{3,2},{4,3},{5,4},{6,5},{7,6},{0,7},{9,8},{10,9},{11,1... | collective-permute-start | bytes 786440 | tf_op jit(solution)/shard_map/ppermute | solution.py:541
  16.8 2.4 %slice-start.1 = ((s8[8388608]{0:T(1024)(128)(4,1)}), s8[4194304]{0:T(1024)(128)(4,1)S(1)}, s32[]{:S(2)}) async-start(s8[8388608]{0:T(1024)(128)(4,1)} %bitcast.124), calls=%async_computation.1 | async-start | bytes 8388608
  17.0 1.3 %copy-start.10 = (bf16[7,7,64,128]{3,2,1,0:T(8,128)(2,1)S(1)}, bf16[7,7,64,128]{3,2,1,0:T(8,128)(2,1)}, u32[]{:S(2)}) copy-start(bf16[7,7,64,128]{3,2,1,0:T(8,128)(2,1)} %param.24) | copy-start | bytes 2408452
  18.3 1.8 %copy-start = (bf16[1,1,512,32,64]{2,4,3,1,0:T(8,128)(2,1)S(1)}, bf16[1,1,512,32,64]{2,4,3,1,0:T(8,128)(2,1)}, u32[]{:S(2)}) copy-start(bf16[1,1,512,32,64]{2,4,3,1,0:T(8,128)(2,1)} %param.14) | copy-start | bytes 6291460
  18.3 1.8 %copy-start.4 = (s32[1,1,512]{2,1,0:T(1,128)S(1)}, s32[1,1,512]{2,1,0:T(1,128)}, u32[]{:S(2)}) copy-start(s32[1,1,512]{2,1,0:T(1,128)} %param.16) | copy-start | bytes 6148
  20.1 13.4 %copy-start.2 = (bf16[512,512]{1,0:T(8,128)(2,1)S(1)}, bf16[512,512]{1,0:T(8,128)(2,1)}, u32[]{:S(2)}) copy-start(bf16[512,512]{1,0:T(8,128)(2,1)} %constant.5.clone.place_ref) | copy-start | bytes 1572868
  20.1 13.4 %copy-start.5 = (f32[64]{0:T(128)S(1)}, f32[64]{0:T(128)}, u32[]{:S(2)}) copy-start(f32[64]{0:T(128)} %param.22) | copy-start | bytes 772
  20.1 13.4 %copy-start.6 = (f32[64]{0:T(128)S(1)}, f32[64]{0:T(128)}, u32[]{:S(2)}) copy-start(f32[64]{0:T(128)} %param.23) | copy-start | bytes 772
  20.1 13.4 %copy-start.7 = (f32[128]{0:T(128)S(1)}, f32[128]{0:T(128)}, u32[]{:S(2)}) copy-start(f32[128]{0:T(128)} %param.25) | copy-start | bytes 1540
  20.2 13.4 %copy-start.8 = (f32[128]{0:T(128)S(1)}, f32[128]{0:T(128)}, u32[]{:S(2)}) copy-start(f32[128]{0:T(128)} %param.26) | copy-start | bytes 1540

commit v2 on v1

--- a/solution.py
+++ b/solution.py
@@ -23,22 +23,34 @@
     return pltpu.CompilerParams(vmem_limit_bytes=VMEM_LIMIT)
 
 
+def turn(v):
+    n = v.shape[1]
+    row = lax.broadcasted_iota(jnp.int32, (n, n), 0)
+    col = lax.broadcasted_iota(jnp.int32, (n, n), 1)
+    eye = jnp.where(row == col, 1.0, 0.0).astype(BF16)
+    return lax.dot_general(eye, v, (((1,), (1,)), ((), ())), preferred_element_type=F32)
+
+
+def spacing(channels):
+    return channels + 8
+
+
 def turn_states(s_ref, turned, distance):
     channels, _, block = s_ref.shape
 
     def body(i, _):
-        for u in range(2):
-            c = i * 2 + u
+        for u in range(4):
+            c = i * 4 + u
             v = s_ref[c]
             if block == distance * 2 and distance % 128 == 0:
                 pair = jnp.concatenate([v[:, :distance], v[:, distance:]], axis=0)
             else:
                 other = pltpu.roll(v.astype(F32), block - distance, 1).astype(BF16)
                 pair = jnp.concatenate([v, other], axis=0)
-            turned[pl.ds(c, distance, stride=channels)] = pair.T[:distance].astype(F32)
-        return 0
-
-    lax.fori_loop(0, channels // 2, body, 0)
+            turned[pl.ds(c, distance, stride=spacing(channels))] = turn(pair)[:distance]
+        return 0
+
+    lax.fori_loop(0, channels // 4, body, 0)
 
 
 def group_slots(g, distance):
@@ -46,9 +58,10 @@
 
 
 def group_product(turned, w_ref, mask, g, channels, distance):
-    start = pl.multiple_of(g * 2 * channels, 2 * channels)
+    apart = spacing(channels)
+    start = pl.multiple_of(g * 2 * apart, 8)
     s = jnp.concatenate(
-        [turned[pl.ds(start, channels)], turned[pl.ds(start + channels, channels)]], axis=1
+        [turned[pl.ds(start, channels)], turned[pl.ds(start + apart, channels)]], axis=1
     ).astype(BF16)
     lhs = jnp.concatenate([s] * PACK, axis=0) * mask
     rhs = jnp.concatenate([w_ref[slot] for slot in group_slots(g, distance)], axis=0)
@@ -102,7 +115,7 @@
                 pl.BlockSpec((n, b, pixels), lambda i, t: (0, 0, 0)),
             ],
             out_specs=[pl.BlockSpec((count // 2, c, pixels), lambda i, t: (0, 0, 0))] * 2,
-            scratch_shapes=[pltpu.VMEM((count, c, pixels), F32), pltpu.VMEM((n // 2 * c, 2 * b), F32)],
+            scratch_shapes=[pltpu.VMEM((count, c, pixels), F32), pltpu.VMEM((n // 2 * spacing(c), 2 * b), F32)],
         ),
         out_shape=[jax.ShapeDtypeStruct((count // 2, c, pixels), BF16)] * 2,
         compiler_params=params(),
@@ -144,7 +157,7 @@
                 pl.BlockSpec((block, b, pixels), lambda i, t, l: (i, 0, 0)),
             ],
             out_specs=pl.BlockSpec((patches, c, pixels), lambda i, t, l: (0, 0, 0)),
-            scratch_shapes=[pltpu.VMEM((block // 2 * c, 2 * b), F32)],
+            scratch_shapes=[pltpu.VMEM((block // 2 * spacing(c), 2 * b), F32)],
         ),
         out_shape=jax.ShapeDtypeStruct((patches, c, pixels), F32),
         compiler_params=params(),
@@ -188,7 +201,7 @@
             part = moved[at : at + channels]
             at += channels
             stacked = jnp.concatenate([part[:, f * npos : (f + 1) * npos] for f in range(4)], axis=0)
-            turned = stacked.astype(BF16).T
+            turned = turn(stacked.astype(BF16)).astype(BF16)
             for rx2 in range(2):
                 for py in range(PH // 2):
                     start = (rx2 * (PH // 2) + py) * wide

time: 65 us -> 64.3 us (0.989)
  Pallas kernels: 48.9 us -> 48.1 us
    pallas_call x1, Pallas kernels: 13.3 us -> 11.8 us  [inner_sums(): pl.pallas_call(functools.partial(inner_kernel, patches // block), grid_sp...]
    pallas_call x1, Pallas kernels: 30.4 us -> 31.7 us  [encode(): pl.pallas_call(functools.partial(encoder_kernel, patch_cols, ci), in_spec...]
  transfers between devices with their start and end apart: 2 -> 2, of which waited for: 0 -> 0; matrix products, arithmetic and copies ran while one was open for 4% -> 4% of each run, Pallas kernels for 21% -> 18%
where the time goes in v2:
time: 64.3 us; the launch traced here: 63.9 us
  Pallas kernels  48.1 us (75%)
  local copies, waits for them, and re-layouts  6.44 us (10%)
  starting transfers between devices  6.11 us (10%)
  other arithmetic  2.08 us (3%)
  between operations  1.16 us (2%)
    pallas_call x1, Pallas kernels, encode(): pl.pallas_call(functools.partial(encoder_kernel, patch_cols, ci), in_spec...  31.7 us
    pallas_call x1, Pallas kernels, inner_sums(): pl.pallas_call(functools.partial(inner_kernel, patches // block), grid_sp...  11.8 us
    unnamed x51, local copies, waits for them, and re-layouts  5.96 us
    pallas_call x1, Pallas kernels, border_sums(): pl.pallas_call(border_kernel, grid_spec=pltpu.PrefetchScalarGridSpec(num_...  4.73 us
    ppermute x1, starting transfers between devices, local(): lax.ppermute(to_west, 'lon', [((i + 1) % nlon, i) for i in range(nlon)])  3.1 us
    ppermute x1, starting transfers between devices, local(): lax.ppermute(to_east, 'lon', [(i, (i + 1) % nlon) for i in range(nlon)])  3.02 us
    concatenate x1, other arithmetic, weights_one(): full = jnp.concatenate(parts, axis=-1)  2.08 us
  transfers between devices with their start and end apart: 2, of which 0 were waited for; matrix products, arithmetic and copies ran while one was open for 4% of the time, Pallas kernels for 18%

profile of v2, /device:TPU:0, one launch (start us, length us, event | category | flops | bytes accessed | tf_op | source)
XLA Modules:
  0.0 63.9 jit_solution(12236809086216738416)
XLA Ops:
  0.0 0.0 copy-start.1
  0.0 1.6 %copy-done.1 = bf16[1,1,128,64,128]{4,3,2,1,0:T(8,128)(2,1)S(1)} copy-done((bf16[1,1,128,64,128]{4,3,2,1,0:T(8,128)(2,1)S(1)}, bf16[1,1,128,64,128]{4,3,2,1,0:T(8,128)(2,1)}, u32[]{:S(2)}) %copy-start.1) | copy-done | bytes 2097176
  1.6 0.0 copy-start.3
  1.6 1.0 %copy-done.3 = bf16[1,1,128,32,64]{2,4,3,1,0:T(8,128)(2,1)S(1)} copy-done((bf16[1,1,128,32,64]{2,4,3,1,0:T(8,128)(2,1)S(1)}, bf16[1,1,128,32,64]{2,4,3,1,0:T(8,128)(2,1)}, u32[]{:S(2)}) %copy-start.3) | copy-done | bytes 524312
  2.6 0.0 copy-start.9
  2.6 0.7 %copy-done.9 = s32[1,1,128]{2,1,0:T(1,128)S(1)} copy-done((s32[1,1,128]{2,1,0:T(1,128)S(1)}, s32[1,1,128]{2,1,0:T(1,128)}, u32[]{:S(2)}) %copy-start.9) | copy-done | bytes 536
  3.3 0.0 slice-start
  3.3 4.7 %border_sums.1 = (bf16[32,32,128]{2,1,0:T(8,128)(2,1)S(1)}, bf16[32,32,128]{2,1,0:T(8,128)(2,1)S(1)}) custom-call(s32[128]{0:T(128)S(1)} %bitcast.136, bf16[32,64,128]{2,1,0:T(8,128)(2,1)S(1)} %bitcast.130, bf16[128,64,128]{2,1,0:T(8,128)(2,1)S(1)} %bitcast.129), custom_call_target="tpu_custom_call" | custom-call | tf_op jit(solution)/shard_map/border_sums/pallas_call | solution.py:108
  8.0 3.0 %collective-permute-start = (bf16[32,32,128]{2,1,0:T(8,128)(2,1)S(1)}, bf16[32,32,128]{2,1,0:T(8,128)(2,1)S(1)}, u32[]{:S(2)}, u32[]{:S(2)}) collective-permute-start(bf16[32,32,128]{2,1,0:T(8,128)(2,1)S(1)} %get-tuple-element.7), channel_id=1, source_target_pairs={{0,1},{1,2},{2,3},{3,4},{4,5},{5,6},{6,7},{7,0},{8,9},{9,10},{10,1... | collective-permute-start | bytes 786440 | tf_op jit(solution)/shard_map/ppermute | solution.py:553
  11.0 3.1 %collective-permute-start.1 = (bf16[32,32,128]{2,1,0:T(8,128)(2,1)S(1)}, bf16[32,32,128]{2,1,0:T(8,128)(2,1)S(1)}, u32[]{:S(2)}, u32[]{:S(2)}) collective-permute-start(bf16[32,32,128]{2,1,0:T(8,128)(2,1)S(1)} %get-tuple-element.8), channel_id=1, source_target_pairs={{1,0},{2,1},{3,2},{4,3},{5,4},{6,5},{7,6},{0,7},{9,8},{10,9},{11,1... | collective-permute-start | bytes 786440 | tf_op jit(solution)/shard_map/ppermute | solution.py:554
  14.1 2.1 %fusion.7 = bf16[12,12,32,256]{3,2,1,0:T(8,128)(2,1)S(1)} fusion(bf16[7,7,32,64]{3,2,1,0:T(8,128)(2,1)} %param.21), kind=kLoop, calls=%fused_computation.13 | loop fusion | flops 23592960 | bytes 2560000 | tf_op jit(solution)/shard_map/concatenate | solution.py:520
  16.2 0.0 slice-start.1
  16.3 0.2 copy.15
  16.5 0.0 copy-start.10
  17.6 0.1 copy-done.10
  17.8 0.0 copy-start
  17.8 0.0 copy-start.4
  17.8 0.1 pad.24
  17.9 0.1 copy.16
  18.0 0.0 slice-done
  18.1 0.6 slice-done.1
  18.7 0.9 %copy-done = bf16[1,1,512,32,64]{2,4,3,1,0:T(8,128)(2,1)S(1)} copy-done((bf16[1,1,512,32,64]{2,4,3,1,0:T(8,128)(2,1)S(1)}, bf16[1,1,512,32,64]{2,4,3,1,0:T(8,128)(2,1)}, u32[]{:S(2)}) %copy-start) | copy-done | bytes 2097176
  19.6 0.0 copy-done.4
  19.6 0.0 copy-start.2
  19.6 0.0 copy-start.5
  19.6 0.0 copy-start.6
  19.6 0.0 copy-start.7
  19.6 0.0 copy-start.8
  19.6 11.8 %inner_sums.1.acc_ref = f32[256,32,128]{2,1,0:T(8,128)S(1)} custom-call(s32[512]{0:T(512)S(1)} %bitcast.131, s32[1]{0:T(128)} %bitcast.123.live_ref, bf16[32,64,512]{2,1,0:T(8,128)(2,1)S(1)} %bitcast.128, bf16[512,64,128]{2,1,0:T(8,128)(2,1)S(1)} %bitcast.126), custom_call_target="tpu_custom_call" | custom-call | tf_op jit(solution)/shard_map/inner_sums/pallas_call | solution.py:150
  31.4 0.0 collective-permute-done.west_ref
  31.4 0.0 collective-permute-done.1.east_ref
  31.4 0.0 copy-done.2
  31.4 0.0 copy-done.5
  31.5 0.0 copy-done.6
  31.5 0.0 copy-done.7
  31.5 0.0 copy-done.8
  31.5 31.7 %encoder.1 = bf16[64,32,128]{2,1,0:T(8,128)(2,1)S(1)} custom-call(f32[256,32,128]{2,1,0:T(8,128)S(1)} %inner_sums.1.acc_ref, bf16[32,32,128]{2,1,0:T(8,128)(2,1)S(1)} %collective-permute-done.west_ref, bf16[32,32,128]{2,1,0:T(8,128)(2,1)S(1)} %collective-permute-done.1.east_ref, bf16[512,512]{1,0:T(8,128)(2,1)S(1)} %copy-done.2, ...), custom_call_target="tpu_custom_call" | custom-call | tf_op jit(solution)/shard_map/encoder/pallas_call | solution.py:484
  63.1 0.8 %copy.43 = bf16[64,32,128]{2,1,0:T(8,128)(2,1)} copy(bf16[64,32,128]{2,1,0:T(8,128)(2,1)S(1)} %encoder.1) | data formatting | bytes 1048576
  (26 shorter events, 0.2 us)
Async XLA Ops:
  0.0 1.6 %copy-start.1 = (bf16[1,1,128,64,128]{4,3,2,1,0:T(8,128)(2,1)S(1)}, bf16[1,1,128,64,128]{4,3,2,1,0:T(8,128)(2,1)}, u32[]{:S(2)}) copy-start(bf16[1,1,128,64,128]{4,3,2,1,0:T(8,128)(2,1)} %param.19) | copy-start | bytes 6291460
  1.6 1.0 %copy-start.3 = (bf16[1,1,128,32,64]{2,4,3,1,0:T(8,128)(2,1)S(1)}, bf16[1,1,128,32,64]{2,4,3,1,0:T(8,128)(2,1)}, u32[]{:S(2)}) copy-start(bf16[1,1,128,32,64]{2,4,3,1,0:T(8,128)(2,1)} %param.18) | copy-start | bytes 1572868
  2.6 0.7 %copy-start.9 = (s32[1,1,128]{2,1,0:T(1,128)S(1)}, s32[1,1,128]{2,1,0:T(1,128)}, u32[]{:S(2)}) copy-start(s32[1,1,128]{2,1,0:T(1,128)} %param.20) | copy-start | bytes 1540
  3.3 14.8 %slice-start = ((s8[8388608]{0:T(1024)(128)(4,1)}), s8[4194304]{0:T(1024)(128)(4,1)S(1)}, s32[]{:S(2)}) async-start(s8[8388608]{0:T(1024)(128)(4,1)} %bitcast.124), calls=%async_computation | async-start | bytes 8388608
  8.0 23.4 %collective-permute-start = (bf16[32,32,128]{2,1,0:T(8,128)(2,1)S(1)}, bf16[32,32,128]{2,1,0:T(8,128)(2,1)S(1)}, u32[]{:S(2)}, u32[]{:S(2)}) collective-permute-start(bf16[32,32,128]{2,1,0:T(8,128)(2,1)S(1)} %get-tuple-element.7), channel_id=1, source_target_pairs={{0,1},{1,2},{2,3},{3,4},{4,5},{5,6},{6,7},{7,0},{8,9},{9,10},{10,1... | collective-permute-start | bytes 786440 | tf_op jit(solution)/shard_map/ppermute | solution.py:553
  11.0 20.4 %collective-permute-start.1 = (bf16[32,32,128]{2,1,0:T(8,128)(2,1)S(1)}, bf16[32,32,128]{2,1,0:T(8,128)(2,1)S(1)}, u32[]{:S(2)}, u32[]{:S(2)}) collective-permute-start(bf16[32,32,128]{2,1,0:T(8,128)(2,1)S(1)} %get-tuple-element.8), channel_id=1, source_target_pairs={{1,0},{2,1},{3,2},{4,3},{5,4},{6,5},{7,6},{0,7},{9,8},{10,9},{11,1... | collective-permute-start | bytes 786440 | tf_op jit(solution)/shard_map/ppermute | solution.py:554
  16.2 2.4 %slice-start.1 = ((s8[8388608]{0:T(1024)(128)(4,1)}), s8[4194304]{0:T(1024)(128)(4,1)S(1)}, s32[]{:S(2)}) async-start(s8[8388608]{0:T(1024)(128)(4,1)} %bitcast.124), calls=%async_computation.1 | async-start | bytes 8388608
  16.5 1.3 %copy-start.10 = (bf16[7,7,64,128]{3,2,1,0:T(8,128)(2,1)S(1)}, bf16[7,7,64,128]{3,2,1,0:T(8,128)(2,1)}, u32[]{:S(2)}) copy-start(bf16[7,7,64,128]{3,2,1,0:T(8,128)(2,1)} %param.24) | copy-start | bytes 2408452
  17.8 1.8 %copy-start = (bf16[1,1,512,32,64]{2,4,3,1,0:T(8,128)(2,1)S(1)}, bf16[1,1,512,32,64]{2,4,3,1,0:T(8,128)(2,1)}, u32[]{:S(2)}) copy-start(bf16[1,1,512,32,64]{2,4,3,1,0:T(8,128)(2,1)} %param.14) | copy-start | bytes 6291460
  17.8 1.8 %copy-start.4 = (s32[1,1,512]{2,1,0:T(1,128)S(1)}, s32[1,1,512]{2,1,0:T(1,128)}, u32[]{:S(2)}) copy-start(s32[1,1,512]{2,1,0:T(1,128)} %param.16) | copy-start | bytes 6148
  19.6 11.8 %copy-start.2 = (bf16[512,512]{1,0:T(8,128)(2,1)S(1)}, bf16[512,512]{1,0:T(8,128)(2,1)}, u32[]{:S(2)}) copy-start(bf16[512,512]{1,0:T(8,128)(2,1)} %constant.5.clone.place_ref) | copy-start | bytes 1572868
  19.6 11.8 %copy-start.5 = (f32[64]{0:T(128)S(1)}, f32[64]{0:T(128)}, u32[]{:S(2)}) copy-start(f32[64]{0:T(128)} %param.22) | copy-start | bytes 772
  19.6 11.9 %copy-start.6 = (f32[64]{0:T(128)S(1)}, f32[64]{0:T(128)}, u32[]{:S(2)}) copy-start(f32[64]{0:T(128)} %param.23) | copy-start | bytes 772
  19.6 11.9 %copy-start.7 = (f32[128]{0:T(128)S(1)}, f32[128]{0:T(128)}, u32[]{:S(2)}) copy-start(f32[128]{0:T(128)} %param.25) | copy-start | bytes 1540
  19.6 11.9 %copy-start.8 = (f32[128]{0:T(128)S(1)}, f32[128]{0:T(128)}, u32[]{:S(2)}) copy-start(f32[128]{0:T(128)} %param.26) | copy-start | bytes 1540

commit v3 on v2

--- a/solution.py
+++ b/solution.py
@@ -81,13 +81,13 @@
     mask = slot_mask(channels, cells)
 
     def body(i, _):
-        prods = [group_product(turned, w_ref, mask, i * 4 + u, channels, distance) for u in range(4)]
+        prods = [group_product(turned, w_ref, mask, i * 8 + u, channels, distance) for u in range(8)]
         for u, prod in enumerate(prods):
-            for k, slot in enumerate(group_slots(i * 4 + u, distance)):
+            for k, slot in enumerate(group_slots(i * 8 + u, distance)):
                 store(base + slot, prod[k * channels : (k + 1) * channels])
         return 0
 
-    lax.fori_loop(0, block // (4 * PACK), body, 0)
+    lax.fori_loop(0, block // (8 * PACK), body, 0)
 
 
 def border_kernel(target_ref, s_ref, w_ref, west_ref, east_ref, acc, turned):
@@ -118,7 +118,7 @@
             scratch_shapes=[pltpu.VMEM((count, c, pixels), F32), pltpu.VMEM((n // 2 * spacing(c), 2 * b), F32)],
         ),
         out_shape=[jax.ShapeDtypeStruct((count // 2, c, pixels), BF16)] * 2,
-        compiler_params=params(),
+        compiler_params=pltpu.CompilerParams(vmem_limit_bytes=60 * 1024 * 1024),
         name="border_sums",
     )(targets, states.transpose(1, 2, 0), weights)
 

time: 64.3 us -> 60.4 us (0.939)
  local copies, waits for them, and re-layouts: 6.44 us -> 4.16 us
  other arithmetic: 2.08 us -> 0.81 us
    pallas_call x1, Pallas kernels: 11.8 us -> 9.27 us  [inner_sums(): pl.pallas_call(functools.partial(inner_kernel, patches // block), grid_sp...]
    unnamed x51 -> x45, local copies, waits for them, and re-layouts: 5.96 us -> 3.69 us
    pallas_call x1, Pallas kernels: 4.73 us -> 6.87 us  [border_sums(): pl.pallas_call(border_kernel, grid_spec=pltpu.PrefetchScalarGridSpec(num_...]
    concatenate x1, other arithmetic: 2.08 us -> 0.81 us  [weights_one(): full = jnp.concatenate(parts, axis=-1)]
  transfers between devices with their start and end apart: 2 -> 2, of which waited for: 0 -> 0; matrix products, arithmetic and copies ran while one was open for 4% -> 2% of each run, Pallas kernels for 18% -> 15%
where the time goes in v3:
time: 60.4 us; the launch traced here: 60.2 us
  Pallas kernels  48 us (79%)
  starting transfers between devices  6.02 us (10%)
  local copies, waits for them, and re-layouts  4.16 us (7%)
  between operations  1.27 us (2%)
  other arithmetic  0.81 us (1%)
    pallas_call x1, Pallas kernels, encode(): pl.pallas_call(functools.partial(encoder_kernel, patch_cols, ci), in_spec...  31.8 us
    pallas_call x1, Pallas kernels, inner_sums(): pl.pallas_call(functools.partial(inner_kernel, patches // block), grid_sp...  9.27 us
    pallas_call x1, Pallas kernels, border_sums(): pl.pallas_call(border_kernel, grid_spec=pltpu.PrefetchScalarGridSpec(num_...  6.87 us
    unnamed x45, local copies, waits for them, and re-layouts  3.69 us
    ppermute x1, starting transfers between devices, local(): lax.ppermute(to_west, 'lon', [((i + 1) % nlon, i) for i in range(nlon)])  3.05 us
    ppermute x1, starting transfers between devices, local(): lax.ppermute(to_east, 'lon', [(i, (i + 1) % nlon) for i in range(nlon)])  2.97 us
  transfers between devices with their start and end apart: 2, of which 0 were waited for; matrix products, arithmetic and copies ran while one was open for 2% of the time, Pallas kernels for 15%

profile of v3, /device:TPU:0, one launch (start us, length us, event | category | flops | bytes accessed | tf_op | source)
XLA Modules:
  0.0 60.2 jit_solution(6616037664484778003)
XLA Ops:
  0.0 0.0 copy-start.9
  0.0 6.9 %border_sums.1 = (bf16[32,32,128]{2,1,0:T(8,128)(2,1)}, bf16[32,32,128]{2,1,0:T(8,128)(2,1)}) custom-call(s32[128]{0:T(128)} %bitcast.161, bf16[32,64,128]{2,1,0:T(8,128)(2,1)} %bitcast.160, bf16[128,64,128]{2,1,0:T(8,128)(2,1)} %bitcast.159), custom_call_target="tpu_custom_call" | custom-call | tf_op jit(solution)/shard_map/border_sums/pallas_call | solution.py:108
  6.9 3.0 %collective-permute-start = (bf16[32,32,128]{2,1,0:T(8,128)(2,1)}, bf16[32,32,128]{2,1,0:T(8,128)(2,1)S(1)}, u32[]{:S(2)}, u32[]{:S(2)}) collective-permute-start(bf16[32,32,128]{2,1,0:T(8,128)(2,1)} %get-tuple-element.7), channel_id=1, source_target_pairs={{0,1},{1,2},{2,3},{3,4},{4,5},{5,6},{6,7},{7,0},{8,9},{9,10},{10,1... | collective-permute-start | bytes 786440 | tf_op jit(solution)/shard_map/ppermute | solution.py:553
  9.8 3.0 %collective-permute-start.1 = (bf16[32,32,128]{2,1,0:T(8,128)(2,1)}, bf16[32,32,128]{2,1,0:T(8,128)(2,1)S(1)}, u32[]{:S(2)}, u32[]{:S(2)}) collective-permute-start(bf16[32,32,128]{2,1,0:T(8,128)(2,1)} %get-tuple-element.8), channel_id=1, source_target_pairs={{1,0},{2,1},{3,2},{4,3},{5,4},{6,5},{7,6},{0,7},{9,8},{10,9},{11,1... | collective-permute-start | bytes 786440 | tf_op jit(solution)/shard_map/ppermute | solution.py:554
  12.9 0.0 copy-done.9
  12.9 0.8 %fusion.7 = bf16[12,12,32,256]{3,2,1,0:T(8,128)(2,1)S(1)} fusion(bf16[7,7,32,64]{3,2,1,0:T(8,128)(2,1)S(1)} %copy-done.9), kind=kLoop, calls=%fused_computation.13 | loop fusion | flops 23592960 | bytes 2560000 | tf_op jit(solution)/shard_map/concatenate | solution.py:520
  13.7 0.0 copy-start.8
  13.7 0.0 copy-start
  13.7 0.2 copy.15
  15.2 0.0 copy-done.8
  15.2 0.0 copy-start.1
  15.2 0.0 copy-start.3
  15.3 0.1 pad.24
  15.4 0.1 copy.16
  15.5 1.9 %copy-done = bf16[1,1,512,64,128]{4,3,2,1,0:T(8,128)(2,1)S(1)} copy-done((bf16[1,1,512,64,128]{4,3,2,1,0:T(8,128)(2,1)S(1)}, bf16[1,1,512,64,128]{4,3,2,1,0:T(8,128)(2,1)}, u32[]{:S(2)}) %copy-start) | copy-done | bytes 8388632
  17.4 0.8 %copy-done.1 = bf16[1,1,512,32,64]{2,4,3,1,0:T(8,128)(2,1)S(1)} copy-done((bf16[1,1,512,32,64]{2,4,3,1,0:T(8,128)(2,1)S(1)}, bf16[1,1,512,32,64]{2,4,3,1,0:T(8,128)(2,1)}, u32[]{:S(2)}) %copy-start.1) | copy-done | bytes 2097176
  18.2 0.0 copy-done.3
  18.2 0.0 copy-start.2
  18.2 0.0 copy-start.4
  18.2 0.0 copy-start.5
  18.2 0.0 copy-start.6
  18.2 0.0 copy-start.7
  18.2 9.3 %inner_sums.1.acc_ref = f32[256,32,128]{2,1,0:T(8,128)S(1)} custom-call(s32[512]{0:T(512)S(1)} %bitcast.127, s32[1]{0:T(128)} %bitcast.123.live_ref, bf16[32,64,512]{2,1,0:T(8,128)(2,1)S(1)} %bitcast.126, bf16[512,64,128]{2,1,0:T(8,128)(2,1)S(1)} %bitcast.124), custom_call_target="tpu_custom_call" | custom-call | tf_op jit(solution)/shard_map/inner_sums/pallas_call | solution.py:150
  27.5 0.0 collective-permute-done.west_ref
  27.5 0.0 collective-permute-done.1.east_ref
  27.6 0.0 copy-done.2
  27.6 0.0 copy-done.4
  27.6 0.0 copy-done.5
  27.6 0.0 copy-done.6
  27.6 0.0 copy-done.7
  27.6 31.8 %encoder.1 = bf16[64,32,128]{2,1,0:T(8,128)(2,1)S(1)} custom-call(f32[256,32,128]{2,1,0:T(8,128)S(1)} %inner_sums.1.acc_ref, bf16[32,32,128]{2,1,0:T(8,128)(2,1)S(1)} %collective-permute-done.west_ref, bf16[32,32,128]{2,1,0:T(8,128)(2,1)S(1)} %collective-permute-done.1.east_ref, bf16[512,512]{1,0:T(8,128)(2,1)S(1)} %copy-done.2, ...), custom_call_target="tpu_custom_call" | custom-call | tf_op jit(solution)/shard_map/encoder/pallas_call | solution.py:484
  59.4 0.8 %copy.43 = bf16[64,32,128]{2,1,0:T(8,128)(2,1)} copy(bf16[64,32,128]{2,1,0:T(8,128)(2,1)S(1)} %encoder.1) | data formatting | bytes 1048576
  (25 shorter events, 0.2 us)
Async XLA Ops:
  0.0 12.9 %copy-start.9 = (bf16[7,7,32,64]{3,2,1,0:T(8,128)(2,1)S(1)}, bf16[7,7,32,64]{3,2,1,0:T(8,128)(2,1)}, u32[]{:S(2)}) copy-start(bf16[7,7,32,64]{3,2,1,0:T(8,128)(2,1)} %param.21) | copy-start | bytes 602116
  6.9 20.7 %collective-permute-start = (bf16[32,32,128]{2,1,0:T(8,128)(2,1)}, bf16[32,32,128]{2,1,0:T(8,128)(2,1)S(1)}, u32[]{:S(2)}, u32[]{:S(2)}) collective-permute-start(bf16[32,32,128]{2,1,0:T(8,128)(2,1)} %get-tuple-element.7), channel_id=1, source_target_pairs={{0,1},{1,2},{2,3},{3,4},{4,5},{5,6},{6,7},{7,0},{8,9},{9,10},{10,1... | collective-permute-start | bytes 786440 | tf_op jit(solution)/shard_map/ppermute | solution.py:553
  9.8 17.7 %collective-permute-start.1 = (bf16[32,32,128]{2,1,0:T(8,128)(2,1)}, bf16[32,32,128]{2,1,0:T(8,128)(2,1)S(1)}, u32[]{:S(2)}, u32[]{:S(2)}) collective-permute-start(bf16[32,32,128]{2,1,0:T(8,128)(2,1)} %get-tuple-element.8), channel_id=1, source_target_pairs={{1,0},{2,1},{3,2},{4,3},{5,4},{6,5},{7,6},{0,7},{9,8},{10,9},{11,1... | collective-permute-start | bytes 786440 | tf_op jit(solution)/shard_map/ppermute | solution.py:554
  13.7 1.5 %copy-start.8 = (bf16[7,7,64,128]{3,2,1,0:T(8,128)(2,1)S(1)}, bf16[7,7,64,128]{3,2,1,0:T(8,128)(2,1)}, u32[]{:S(2)}) copy-start(bf16[7,7,64,128]{3,2,1,0:T(8,128)(2,1)} %param.24) | copy-start | bytes 2408452
  13.7 3.7 %copy-start = (bf16[1,1,512,64,128]{4,3,2,1,0:T(8,128)(2,1)S(1)}, bf16[1,1,512,64,128]{4,3,2,1,0:T(8,128)(2,1)}, u32[]{:S(2)}) copy-start(bf16[1,1,512,64,128]{4,3,2,1,0:T(8,128)(2,1)} %param.15) | copy-start | bytes 25165828
  15.2 3.0 %copy-start.1 = (bf16[1,1,512,32,64]{2,4,3,1,0:T(8,128)(2,1)S(1)}, bf16[1,1,512,32,64]{2,4,3,1,0:T(8,128)(2,1)}, u32[]{:S(2)}) copy-start(bf16[1,1,512,32,64]{2,4,3,1,0:T(8,128)(2,1)} %param.14) | copy-start | bytes 6291460
  15.2 3.0 %copy-start.3 = (s32[1,1,512]{2,1,0:T(1,128)S(1)}, s32[1,1,512]{2,1,0:T(1,128)}, u32[]{:S(2)}) copy-start(s32[1,1,512]{2,1,0:T(1,128)} %param.16) | copy-start | bytes 6148
  18.2 9.4 %copy-start.2 = (bf16[512,512]{1,0:T(8,128)(2,1)S(1)}, bf16[512,512]{1,0:T(8,128)(2,1)}, u32[]{:S(2)}) copy-start(bf16[512,512]{1,0:T(8,128)(2,1)} %constant.5.clone.place_ref) | copy-start | bytes 1572868
  18.2 9.4 %copy-start.4 = (f32[64]{0:T(128)S(1)}, f32[64]{0:T(128)}, u32[]{:S(2)}) copy-start(f32[64]{0:T(128)} %param.22) | copy-start | bytes 772
  18.2 9.4 %copy-start.5 = (f32[64]{0:T(128)S(1)}, f32[64]{0:T(128)}, u32[]{:S(2)}) copy-start(f32[64]{0:T(128)} %param.23) | copy-start | bytes 772
  18.2 9.4 %copy-start.6 = (f32[128]{0:T(128)S(1)}, f32[128]{0:T(128)}, u32[]{:S(2)}) copy-start(f32[128]{0:T(128)} %param.25) | copy-start | bytes 1540
  18.2 9.4 %copy-start.7 = (f32[128]{0:T(128)S(1)}, f32[128]{0:T(128)}, u32[]{:S(2)}) copy-start(f32[128]{0:T(128)} %param.26) | copy-start | bytes 1540
